TPU v7x, 128 devices: a whole 4x4x4 slice. The times are simulated.
128 devices in a mesh: lon: 16 (over y, z), lat: 4 (over x_lo, core), lev: 2 (over x_hi).
Axes of the slice: x: 4 (x_hi: 2, x_lo: 2; x = x_hi * 2 + x_lo), y: 4, z: 4, core: 2. Of those that a mesh axis runs over, the one named last changes fastest.
Arguments:
- tracers: float32 [4, 6, 1800, 2048], P(None, 'lev', 'lat', 'lon'), parts along dimension 1, may hold values from -6 to 6
- zonal_courant: float32 [6, 1800, 2048], P('lev', 'lat', 'lon'), parts along dimension 0, as said below
- merid_courant: float32 [6, 1800, 2048], P('lev', 'lat', 'lon'), parts along dimension 0, may hold values from -0.25 to 0.25
Outputs:
- advected: float32 [4, 6, 1800, 2048], P(None, 'lev', 'lat', 'lon'), parts along dimension 1
There are 2 independent parts, one for each index of `lev`. A program takes and returns all parts, laid end to end along the dimension named above; each array names one. Nothing has to cross between parts.
Inputs may be any that keep to these rules, and one draw needn't show every extreme that they name: `zonal_courant`: magnitudes are at most 0.25 outside the first 224 and last 224 rows of the globe and at most 1 inside them.
All inputs are finite; a program needn't handle non-finite values.
Results may differ from a plain program's by a relative error of at most 0.0003.
Values sent between devices are 32-bit elements; how exact they have to be, the bound alone decides.
No kernel may reach another device: no remote copies, remote signals or barrier semaphores. Data moves between devices by JAX's collectives and lax.ppermute only.
A program may use at most 128 MiB of HBM per device.

v0:
```python
import functools

import jax
import jax.numpy as jnp
import numpy as np
from jax import lax
from jax.experimental import pallas as pl
from jax.experimental.pallas import tpu as pltpu
from jax.sharding import PartitionSpec as P

FIELDS, LEVELS = 4, 3
NSUB, NSTEPS, PCAP = 4, 3, 224
BANDS, LOOP = 4, 16
ROWS, LON = 450, 128
GLOBE = ROWS * BANDS
CHUNKS, TILE_STEP = 42, 114
TILES = ((0, 1), (3, 2))
SHIFT_NORTH, SHIFT = 12, 6
E_OWN, E_ROWS = 24, 512
WIDE, NARROW, WIDE_Z, WIDE_M, NARROW_Z, NARROW_M = 24, 6, 23, 16, 5, 4
PAYLOAD = 3 * WIDE + 3 * NARROW + WIDE_Z + WIDE_M + NARROW_Z + NARROW_M
RIM = 24
KEEP, EDGE = 10, 32
INNER_COLS = LON + 16
VMEM_BYTES = 24 * 2**20


def lane_tables():
    band = np.arange(BANDS).reshape(-1, 1, 1, 1, 1)
    tile = np.array(TILES).reshape(1, 2, 1, 2, 1)[:, :, :, np.arange(8) % 2]
    k = np.arange(3).reshape(1, 1, 3, 1, 1)
    chunk = (np.arange(128) % CHUNKS).reshape(1, 1, 1, 1, -1)
    shift = np.where(band == BANDS - 1, SHIFT_NORTH, SHIFT)
    row = band * ROWS + TILE_STEP * tile + 3 * chunk + k - shift
    face = np.where(row % GLOBE == 0, 0.0, np.abs(np.sin(np.pi * row / GLOBE)))
    cell = np.abs(np.sin(np.pi * (row + 0.5) / GLOBE))
    group = np.arange(2).reshape(1, 2, 1, 1, 1)
    polar = (band == 0) & (group == 0) | (band == BANDS - 1) & (group == 1)
    cap = polar & ((row < PCAP) | (row >= GLOBE - PCAP))
    kinds = [face / 6.0, 1.0 / cell, np.where(cap, 1.0 / NSUB, 1.0) / 6.0, cap]
    return np.stack([np.broadcast_to(x, row.shape) for x in kinds], axis=1).astype(np.float32)


def row_payload_kernel(t_hbm, z_hbm, m_hbm, u_ref, v_ref, z_ref, m_ref, rim_ref, sems):
    even = lax.axis_index("lat") % 2 == 0
    last = ROWS * FIELDS - RIM
    copies = [
        pltpu.make_async_copy(z_hbm, z_ref, sems.at[0]),
        pltpu.make_async_copy(m_hbm, m_ref, sems.at[1]),
        pltpu.make_async_copy(t_hbm.at[:, pl.ds(0, RIM), :], rim_ref.at[0], sems.at[2]),
        pltpu.make_async_copy(t_hbm.at[:, pl.ds(last, RIM), :], rim_ref.at[1], sems.at[3]),
    ]
    for copy in copies:
        copy.start()
    for copy in copies:
        copy.wait()

    def put(l, first, south, north):
        u_ref[l, first : first + south.shape[0]] = jnp.where(even, north, south)
        v_ref[l, first : first + south.shape[0]] = jnp.where(even, south, north)

    for l in range(LEVELS):
        put(l, 0, rim_ref[0, l], rim_ref[1, l])
        put(l, RIM, z_ref[l, :8], z_ref[l, ROWS - 8 :])
        put(l, RIM + 8, m_ref[l, :8], m_ref[l, ROWS - 8 :])


def row_payload(tracers, zonal, merid):
    shapes = [(LEVELS, RIM + 16, LON)] * 2 + [(LEVELS, ROWS, LON)] * 2
    return pl.pallas_call(
        row_payload_kernel,
        out_shape=[pltpu.VMEM(shape, jnp.float32) for shape in shapes],
        in_specs=[pl.BlockSpec(memory_space=pltpu.HBM)] * 3,
        out_specs=[pl.BlockSpec(memory_space=pltpu.VMEM)] * len(shapes),
        scratch_shapes=[pltpu.VMEM((2, LEVELS, RIM, LON), jnp.float32), pltpu.SemaphoreType.DMA((4,))],
        compiler_params=pltpu.CompilerParams(vmem_limit_bytes=8 * 2**20),
        name="row_payload",
    )(*[pltpu.with_memory_space_constraint(x, pltpu.HBM) for x in (tracers, zonal, merid)])


def pack_side(side, band, t_ref, e_ref, d_ref, cz_ref, cm_ref):
    base = jnp.where(band == BANDS - 1, E_OWN - SHIFT_NORTH, E_OWN - SHIFT)
    sub = lax.broadcasted_iota(jnp.int32, (8, 128), 0)

    def packed(ref, image, start, per_row):
        x, y, z = (ref[image + l, pl.ds(start - 6 * per_row * l, 48, stride=3 * per_row), :] for l in range(3))
        rows = [x[:40], jnp.where(sub < 2, x[40:], y[:8]), y[8:40], jnp.where(sub < 4, y[40:], z[:8]), z[8:]]
        return jnp.concatenate(rows, axis=0).T

    for g in range(2):
        for k in range(3):
            start = base + TILE_STEP * TILES[g][side] + k
            for f in range(FIELDS):
                d_ref[g * 3 + k, pl.ds(2 * f + side, LON, stride=8), :] = packed(t_ref, 0, start * FIELDS + f, FIELDS)
            cz_ref[g, pl.ds(2 * k + side, LON, stride=8), :] = packed(e_ref, 0, start, 1)
            cm_ref[g, pl.ds(2 * k + side, LON, stride=8), :] = packed(e_ref, LEVELS, start, 1)


def pack_middle_kernel(t_hbm, z_ref, m_ref, after_ref, t_ref, e_ref, d_ref, cz_ref, cm_ref, sems):
    copies = []
    for l in range(LEVELS):
        own = t_ref.at[l, pl.ds(E_OWN * FIELDS, ROWS * FIELDS), :]
        copies.append(pltpu.make_async_copy(t_hbm.at[l], own, sems.at[l]))
        copies[l].start()
    north_end = E_OWN + ROWS
    for l in range(LEVELS):
        t_ref[l, : 4 * E_OWN] = jnp.zeros((4 * E_OWN, LON), jnp.float32)
        t_ref[l, 4 * north_end :] = jnp.zeros((4 * (E_ROWS - north_end), LON), jnp.float32)
        for i, ref in ((l, z_ref), (LEVELS + l, m_ref)):
            e_ref[i, :E_OWN] = jnp.zeros((E_OWN, LON), jnp.float32)
            e_ref[i, E_OWN:north_end] = ref[l]
            e_ref[i, north_end:] = jnp.zeros((E_ROWS - north_end, LON), jnp.float32)
    for copy in copies:
        copy.wait()
    pack_side(1, lax.axis_index("lat"), t_ref, e_ref, d_ref, cz_ref, cm_ref)


ROW_SHAPES = [(LEVELS, E_ROWS * FIELDS, LON), (2 * LEVELS, E_ROWS, LON)]
CELL_SHAPES = [(6, INNER_COLS * 8, 128), (2, (LON + 1) * 8, 128), (2, (LON + 1) * 8, 128)]


def pack_middle(tracers, zonal, merid, after):
    shapes = ROW_SHAPES + CELL_SHAPES
    args = [pltpu.with_memory_space_constraint(tracers, pltpu.HBM)]
    args += [pltpu.with_memory_space_constraint(x, pltpu.VMEM) for x in (zonal, merid, after)]
    return pl.pallas_call(
        pack_middle_kernel,
        out_shape=[pltpu.VMEM(shape, jnp.float32) for shape in shapes],
        in_specs=[pl.BlockSpec(memory_space=pltpu.HBM)] + [pl.BlockSpec(memory_space=pltpu.VMEM)] * 3,
        out_specs=[pl.BlockSpec(memory_space=pltpu.VMEM)] * len(shapes),
        scratch_shapes=[pltpu.SemaphoreType.DMA((LEVELS,))],
        compiler_params=pltpu.CompilerParams(vmem_limit_bytes=8 * 2**20),
        name="pack_middle",
    )(*args)


def pack_rims_kernel(t_in, e_in, d_in, cz_in, cm_in, ru, rv, t_ref, e_ref, d_ref, cz_ref, cm_ref, sw_ref, se_ref):
    band = lax.axis_index("lat")
    even = band % 2 == 0
    north_end = E_OWN + ROWS
    for l in range(LEVELS):
        u, v = ru[l, :RIM], rv[l, :RIM]
        t_ref[l, 4 * E_OWN - RIM : 4 * E_OWN] = jnp.where(even, v, u)
        t_ref[l, 4 * north_end : 4 * north_end + RIM] = jnp.where(even, u, v)
        for i, at in ((l, RIM), (LEVELS + l, RIM + 8)):
            u, v = ru[l, at : at + 8], rv[l, at : at + 8]
            e_ref[i, E_OWN - 8 : E_OWN] = jnp.where(even, v, u)
            e_ref[i, north_end : north_end + 8] = jnp.where(even, u, v)

    def mirrored(start, t_start):
        for l in range(LEVELS):
            for h in range(RIM // 4):
                t_ref[l, t_start + 4 * h : t_start + 4 * (h + 1)] = rv[l, RIM - 4 * (h + 1) : RIM - 4 * h]
            for h in range(8):
                e_ref[l, start + h : start + h + 1] = rv[l, RIM + 7 - h : RIM + 8 - h]
                if h > 0:
                    e_ref[LEVELS + l, start + h : start + h + 1] = -rv[l, RIM + 16 - h : RIM + 17 - h]
                else:
                    e_ref[LEVELS + l, start : start + 1] = jnp.zeros((1, LON), jnp.float32)

    @pl.when(band == 0)
    def _():
        mirrored(E_OWN - 8, 4 * E_OWN - RIM)

    @pl.when(band == BANDS - 1)
    def _():
        mirrored(north_end, 4 * north_end)

    pack_side(0, band, t_ref, e_ref, d_ref, cz_ref, cm_ref)
    wide = jnp.where(band == BANDS - 1, 1, 0)
    thin = 1 - wide

    def payload(out, east):
        at = 0

        def put(ref, index, width):
            nonlocal at
            first = LON - width if east else 0
            out[pl.ds(at * 8, width * 8), :] = ref[index, pl.ds(first * 8, width * 8), :]
            at += width

        for k in range(3):
            put(d_ref, wide * 3 + k, WIDE)
        for k in range(3):
            put(d_ref, thin * 3 + k, NARROW)
        put(cz_ref, wide, WIDE_Z)
        put(cm_ref, wide, WIDE_M)
        put(cz_ref, thin, NARROW_Z)
        put(cm_ref, thin, NARROW_M)

    payload(sw_ref, False)
    payload(se_ref, True)


def pack_rims(middle, ru, rv):
    shapes = ROW_SHAPES + CELL_SHAPES + [(PAYLOAD * 8, 128)] * 2
    return vmem_call(pack_rims_kernel, shapes, [], "pack_rims", {i: i for i in range(5)})(*middle, ru, rv)[2:]


def vmem_call(kernel, shapes, scratch, name, aliases=None):
    vmem = pl.BlockSpec(memory_space=pltpu.VMEM)

    def call(*args):
        return pl.pallas_call(
            kernel,
            out_shape=[pltpu.VMEM(shape, jnp.float32) for shape in shapes],
            in_specs=[vmem] * len(args),
            out_specs=[vmem] * len(shapes),
            scratch_shapes=scratch,
            input_output_aliases=aliases or {},
            compiler_params=pltpu.CompilerParams(vmem_limit_bytes=VMEM_BYTES),
            name=name,
        )(*[pltpu.with_memory_space_constraint(x, pltpu.VMEM) for x in args])

    return call


def upwind(c, a, b, d, e, b3, d3):
    s = b + d
    return c * ((s + s) + jnp.where(c > 0, b3 - a, d3 - e))


def block(ref, index, first, count):
    return ref[index, pl.ds(pl.multiple_of(first * 8, 8), count * 8), :].reshape(count, 8, 128)


def put_block(ref, index, first, value):
    count = value.shape[0]
    ref[index, pl.ds(pl.multiple_of(first * 8, 8), count * 8), :] = value.reshape(count * 8, 128)


def columns(ref, index, first, count):
    return ref.at[index, pl.ds(pl.multiple_of(first * 8, 8), count * 8), :]


def side_one():
    return lax.broadcasted_iota(jnp.int32, (8, 128), 0) % 2 == 1


def roll(x, steps):
    return pltpu.roll(x.reshape(-1, 128), steps, 1).reshape(x.shape)


def spread(source, source_at, out, out_at, scale, first, chunks, masked_at=None, masks=None):
    odd = side_one()

    def body(j, carry):
        for u in range(8):
            i = first + j * 8 + u
            for k in range(3):
                low = source[source_at, pl.ds(i * 8 + 2 * k, 1), :]
                high = source[source_at, pl.ds(i * 8 + 2 * k + 1, 1), :]
                both = jnp.where(odd, jnp.broadcast_to(high, (8, 128)), jnp.broadcast_to(low, (8, 128))) * scale[k]
                put_block(out, out_at + k, i, both[None])
                if masks is not None:
                    put_block(out, masked_at + k, i, (both * masks[k])[None])
        return carry

    lax.fori_loop(0, chunks, body, 0)


def sweeps(s_ref, c_ref, r_ref, count, unroll, zonal=(), meridional=(), inverse=None, band=None, ahead=True):
    def begin(at, c_at, first):
        p = block(s_ref, at, first - 2, 4)
        flux = upwind(block(c_ref, c_at, first, 1)[0], p[0], p[1], p[2], p[3], 3.0 * p[1], 3.0 * p[2])
        return flux[None], p[1:2]

    if band is not None:
        north = band == BANDS - 1
        turn = jnp.where(north, 38, 90)
        chunk = jnp.where(north, CHUNKS - 1, 0)
        k_first = jnp.where(north, 1, 0)
        lane = lax.broadcasted_iota(jnp.int32, (8, 128), 1)
        hit = side_one() & ((lane == chunk) | (lane == chunk + CHUNKS) | (lane == chunk + 2 * CHUNKS))
        hits = [hit & (k_first <= k) & (k <= k_first + 1) for k in range(3)]

    def prepared(n, at, i):
        p = [block(s_ref, at + k, i, unroll) for k in range(3)]
        moves = [roll(p[1], 1), roll(p[2], 1), roll(p[0], 127)]
        if band is not None:
            moves.extend(roll(x, turn) for x in p)
        return [(r_ref, n * 6 + slot, i, value) for slot, value in enumerate(moves)]

    def store(results):
        for ref, where, i, value in results:
            put_block(ref, where, i, value)

    if ahead:
        for n, (at, c_at, first) in enumerate(meridional):
            store(prepared(n, at, first))

    def body(j, carry):
        results, after, begun, moved = [], [], [], []
        for n, (at, c_at, first) in enumerate(meridional):
            i = first + j * unroll
            p = [block(s_ref, at + k, i, unroll) for k in range(3)]
            if ahead:
                moves = [block(r_ref, n * 6 + slot, i, unroll) for slot in range(3 if band is None else 6)]
                store(prepared(n, at, i + unroll))
            else:
                moves = [value for _, _, _, value in prepared(n, at, i)]
            c0, below, twice_below = block(c_ref, c_at, i, unroll), moves[0], moves[1]
            t0 = 3.0 * p[0]
            f0 = upwind(c0, below, twice_below, p[0], p[1], 3.0 * twice_below, t0)
            begun.append((i, p, t0, f0, roll(f0, 127), twice_below, moves[2]))
            moved.extend(moves[3:])
        for (at, c_at, _), (i, (p0, p1, p2), t0, f0, f0_above, p2_below, p0_above) in zip(meridional, begun, strict=True):
            c1, c2 = (block(c_ref, c_at + k, i, unroll) for k in (1, 2))
            t1, t2 = 3.0 * p1, 3.0 * p2
            f1 = upwind(c1, p2_below, p0, p1, p2, t0, t1)
            f2 = upwind(c2, p0, p1, p2, p0_above, t1, t2)
            results.append((s_ref, at, i, p0 - (f1 - f0) * inverse[0]))
            results.append((s_ref, at + 1, i, p1 - (f2 - f1) * inverse[1]))
            results.append((s_ref, at + 2, i, p2 - (f0_above - f2) * inverse[2]))
        for n, (at, c_at, first) in enumerate(zonal):
            i = first + j * unroll
            for k in range(3):
                flux_before, before = carry[n * 3 + k]
                p = jnp.concatenate([before, block(s_ref, at + k, i, unroll + 2)], axis=0)
                c = block(c_ref, c_at + k, i + 1, unroll)
                p3 = 3.0 * p[1 : unroll + 2]
                flux = upwind(c, p[:unroll], p[1 : unroll + 1], p[2 : unroll + 2], p[3:], p3[:-1], p3[1:])
                west = jnp.concatenate([flux_before, flux[:-1]], axis=0)
                value = p[1 : unroll + 1] - (flux - west)
                if band is not None:
                    value = jnp.where(hits[k], moved[n * 3 + k], value)
                results.append((s_ref, at + k, i, value))
                after.append((flux[-1:], p[unroll : unroll + 1]))
        store(results)
        return tuple(after)

    carry = tuple(begin(at + k, c_at + k, first) for at, c_at, first in zonal for k in range(3))
    if count == 1:
        body(0, carry)
    else:
        lax.fori_loop(0, count, body, carry)


ZONAL_WIDE, ZONAL_MASKED, ZONAL_THIN, MERID_WIDE, MERID_THIN, C_SIZE = 0, 3, 6, 9, 12, 15


def spread_all(tab, band, wide, thin, out, base, zonal, merid, spans):
    for g, span, zonal_at, merid_at in ((wide, spans[0], ZONAL_WIDE, MERID_WIDE), (thin, spans[1], ZONAL_THIN, MERID_THIN)):
        scale, weight, cap = ([tab[band, kind, g, k] for k in range(3)] for kind in (2, 0, 3))
        masked = (base + ZONAL_MASKED, cap) if g is wide else ()
        spread(zonal[0], zonal[1] + g, out, base + zonal_at, scale, *span, *masked)
        spread(merid[0], merid[1] + g, out, base + merid_at, weight, *spans[2])


def keep(state_ref, s_ref, cycle, group):
    edge = 8 * cycle
    for k in range(3):
        i = group * 3 + k
        put_block(state_ref, cycle * 6 + i, 0, block(s_ref, i, edge, KEEP))
        put_block(state_ref, cycle * 6 + i, KEEP, block(s_ref, i, LON - edge - KEEP, KEEP))


def inner_kernel(tab, d_ref, cz_ref, cm_ref, s_ref, state_ref, step_ref, c_ref, r_ref):
    band = lax.axis_index("lat")
    is_cap = (band == 0) | (band == BANDS - 1)
    wide = jnp.where(band == BANDS - 1, 1, 0)
    thin = 1 - wide
    at_wide, at_thin = wide * 3, thin * 3
    inverse_wide, inverse_thin = ([tab[band, 1, g, k] for k in range(3)] for g in (wide, thin))
    spread_all(tab, band, wide, thin, c_ref, 0, (cz_ref, 0), (cm_ref, 0), ((0, LON // 8), (8, LON // 8 - 1), (8, LON // 8 - 2)))
    keep(state_ref, s_ref, 0, wide)
    keep(state_ref, s_ref, 0, thin)
    sweeps(s_ref, c_ref, r_ref, LON // 16, 16, [(at_wide, ZONAL_WIDE, 2)])

    for cycle in range(NSTEPS):
        edge = 8 * (cycle + 1)
        kept = LON - 2 * edge

        @pl.when(is_cap)
        def _(cycle=cycle):
            for sub in range(1, NSUB + 1):
                low = 2 * (NSUB * cycle + sub)
                if sub > 1:
                    width = LON - 2 * low
                    unroll = max(n for n in range(8, 31) if width % n == 0)
                    sweeps(s_ref, c_ref, r_ref, width // unroll, unroll, [(at_wide, ZONAL_MASKED, low)])
                if sub < NSUB:
                    for k in range(3):
                        at = (cycle * 3 + sub - 1) * 3 + k
                        put_block(step_ref, at, 0, block(s_ref, at_wide + k, low, 4))
                        put_block(step_ref, at, 4, block(s_ref, at_wide + k, LON - low - 4, 4))

        beside = band if cycle == 0 else None
        sweeps(s_ref, c_ref, r_ref, kept // 16, 16, [(at_thin, ZONAL_THIN, edge)], [(at_wide, MERID_WIDE, edge)], inverse_wide, beside)
        if cycle < NSTEPS - 1:
            keep(state_ref, s_ref, cycle + 1, wide)
            then = [(at_wide, ZONAL_WIDE, edge + 2)]
        else:
            then = []
        sweeps(s_ref, c_ref, r_ref, kept // 16, 16, then, [(at_thin, MERID_THIN, edge)], inverse_thin)
        if cycle < NSTEPS - 1:
            keep(state_ref, s_ref, cycle + 1, thin)


def run_inner(table, cells, cz, cm):
    shapes = [(6, INNER_COLS * 8, 128), (18, 2 * KEEP * 8, 128), (27, 64, 128)]
    scratch = [pltpu.VMEM((n, INNER_COLS * 8, 128), jnp.float32) for n in (C_SIZE, 6)]
    return vmem_call(inner_kernel, shapes, scratch, "inner_columns", {1: 0})(table, cells, cz, cm)


def outer_kernel(tab, cz_ref, cm_ref, rw_ref, re_ref, done_ref, state_ref, step_ref, out_hbm, s_ref, cu_ref, c_ref, w_ref, o_ref, out_sem):
    band = lax.axis_index("lat")
    is_cap = (band == 0) | (band == BANDS - 1)
    wide = jnp.where(band == BANDS - 1, 1, 0)
    thin = 1 - wide
    for g in range(2):
        for kind, own in ((0, cz_ref), (1, cm_ref)):
            put_block(cu_ref, kind * 2 + g, EDGE, block(own, g, 0, EDGE))
            put_block(cu_ref, 4 + kind * 2 + g, 0, block(own, g, LON - EDGE, EDGE))
    for side, recv in ((0, rw_ref), (1, re_ref)):
        at = 0
        plan = [(s_ref, side * 6 + wide * 3 + k, WIDE) for k in range(3)]
        plan += [(s_ref, side * 6 + thin * 3 + k, NARROW) for k in range(3)]
        plan += [(cu_ref, side * 4 + wide, WIDE_Z), (cu_ref, side * 4 + 2 + wide, WIDE_M)]
        plan += [(cu_ref, side * 4 + thin, NARROW_Z), (cu_ref, side * 4 + 2 + thin, NARROW_M)]
        for ref, index, width in plan:
            first = EDGE if side else EDGE - width
            put_block(ref, index, first, recv[at * 8 : (at + width) * 8, :].reshape(width, 8, 128))
            at += width

    def take(cycle, group):
        edge = 8 * cycle
        for k in range(3):
            i = group * 3 + k
            put_block(s_ref, i, EDGE + edge, block(state_ref, cycle * 6 + i, 0, KEEP))
            put_block(s_ref, 6 + i, EDGE - edge - KEEP, block(state_ref, cycle * 6 + i, KEEP, KEEP))

    def places(at, c_at, first):
        return [(side * 6 + at, side * C_SIZE + c_at, first[side]) for side in range(2)]

    def sweep(zonal, meridional=(), inverse=None, beside=None):
        sweeps(s_ref, c_ref, None, 2, 12, zonal, meridional, inverse, beside, ahead=False)

    def first_zonal(cycle):
        low = jnp.where(is_cap, 8 * cycle + 2, 8 * cycle + 8)
        return places(at_wide, ZONAL_WIDE, (EDGE - WIDE + low, EDGE - low))

    at_wide, at_thin = wide * 3, thin * 3
    inverse_wide, inverse_thin = ([tab[band, 1, g, k] for k in range(3)] for g in (wide, thin))
    for side in range(2):
        near = EDGE - WIDE + (0 if side else 8)
        spans = ((EDGE - WIDE, 6 if side else 7), (near, 6), (near, 5))
        spread_all(tab, band, wide, thin, c_ref, side * C_SIZE, (cu_ref, side * 4), (cu_ref, side * 4 + 2), spans)
    take(0, wide)
    take(0, thin)
    sweep(first_zonal(0))

    for cycle in range(NSTEPS):
        edge = 8 * (cycle + 1)
        first = (EDGE - WIDE + edge, EDGE - edge)

        @pl.when(is_cap)
        def _(cycle=cycle):
            for sub in range(1, NSUB + 1):
                low = 2 * (NSUB * cycle + sub)
                if sub > 1:
                    sweep(places(at_wide, ZONAL_MASKED, (EDGE - WIDE + low, EDGE - low)))
                if sub < NSUB:
                    for k in range(3):
                        at = (cycle * 3 + sub - 1) * 3 + k
                        put_block(s_ref, at_wide + k, EDGE + low, block(step_ref, at, 0, 4))
                        put_block(s_ref, 6 + at_wide + k, EDGE - low - 4, block(step_ref, at, 4, 4))

        beside = band if cycle == 0 else None
        sweep(places(at_thin, ZONAL_THIN, first), places(at_wide, MERID_WIDE, first), inverse_wide, beside)
        if cycle < NSTEPS - 1:
            take(cycle + 1, wide)
            then = first_zonal(cycle + 1)
        else:
            then = []
        sweep(then, places(at_thin, MERID_THIN, first), inverse_thin)
        if cycle < NSTEPS - 1:
            take(cycle + 1, thin)

    north = band == BANDS - 1
    shift = jnp.where(north, SHIFT_NORTH, SHIFT)

    def write_rows(tile, act):
        for is_this, shift_here in ((north, SHIFT_NORTH), (jnp.logical_not(north), SHIFT)):
            low = max(0, TILE_STEP * tile + 6 - shift_here)
            high = min(ROWS, TILE_STEP * (tile + 1) + 6 - shift_here)

            @pl.when(is_this)
            def _(low=low, high=high):
                for l in range(LEVELS):
                    rows = (high - low) * FIELDS
                    source = o_ref.at[l, pl.ds((8 + low) * FIELDS, rows), :]
                    act(pltpu.make_async_copy(source, out_hbm.at[l, pl.ds(low * FIELDS, rows), :], out_sem))

    for g in range(2):
        for side in range(2):
            tile = TILES[g][side]
            for k in range(3):
                for f in range(FIELDS):
                    at, row = g * 3 + k, 2 * f + side
                    west = s_ref[at, pl.ds(EDGE * 8 + row, WIDE, stride=8), :]
                    inner = done_ref[at, pl.ds(WIDE * 8 + row, LON - 2 * WIDE, stride=8), :]
                    east = s_ref[6 + at, pl.ds((EDGE - WIDE) * 8 + row, WIDE, stride=8), :]
                    w_ref[f] = jnp.concatenate([west, inner, east], axis=0).T
                    for l in range(LEVELS):
                        start = (8 + TILE_STEP * tile + 6 + k - shift) * FIELDS + f
                        o_ref[l, pl.ds(start, 38, stride=3 * FIELDS), :] = w_ref[f, pl.ds(CHUNKS * l + 2, 38), :]
            write_rows(tile, lambda copy: copy.start())
    for tile in range(4):
        write_rows(tile, lambda copy: copy.wait())


def run_outer(table, cz, cm, from_west, from_east, done, state, step):
    args = [pltpu.with_memory_space_constraint(x, pltpu.VMEM) for x in (table, cz, cm, from_west, from_east, done, state, step)]
    return pl.pallas_call(
        outer_kernel,
        out_shape=jax.ShapeDtypeStruct((LEVELS, ROWS * FIELDS, LON), jnp.float32),
        in_specs=[pl.BlockSpec(memory_space=pltpu.VMEM)] * len(args),
        out_specs=pl.BlockSpec(memory_space=pl.ANY),
        scratch_shapes=[
            pltpu.VMEM((12, 2 * EDGE * 8, 128), jnp.float32),
            pltpu.VMEM((8, 2 * EDGE * 8, 128), jnp.float32),
            pltpu.VMEM((2 * C_SIZE, 2 * EDGE * 8, 128), jnp.float32),
            pltpu.VMEM((FIELDS, 128, 128), jnp.float32),
            pltpu.VMEM((LEVELS, 472 * FIELDS, LON), jnp.float32),
            pltpu.SemaphoreType.DMA,
        ],
        compiler_params=pltpu.CompilerParams(vmem_limit_bytes=VMEM_BYTES),
        name="outer_columns",
    )(*args)


def shards(table, tracers, zonal, merid):
    tracers = tracers.transpose(1, 2, 0, 3).reshape(LEVELS, ROWS * FIELDS, LON)
    su, sv, zonal, merid = row_payload(tracers, zonal, merid)
    middle = pack_middle(tracers, zonal, merid, su)
    within, beyond = [], []
    for lon in range(LOOP):
        for band in range(BANDS):
            within.append((lon * BANDS + band, lon * BANDS + (band ^ 1)))
            if band in (0, BANDS - 1):
                target = (lon + LOOP // 2) % LOOP * BANDS + band
            else:
                target = lon * BANDS + (3 - band)
            beyond.append((lon * BANDS + band, target))
    ru = lax.ppermute(su, ("lon", "lat"), within)
    rv = lax.ppermute(sv, ("lon", "lat"), beyond)
    cells, cz, cm, to_west, to_east = pack_rims(middle, ru, rv)
    from_east = lax.ppermute(to_west, "lon", [(i, (i - 1) % LOOP) for i in range(LOOP)])
    from_west = lax.ppermute(to_east, "lon", [(i, (i + 1) % LOOP) for i in range(LOOP)])
    done, state, step = run_inner(table, cells, cz, cm)
    advected = run_outer(table, cz, cm, from_west, from_east, done, state, step)
    return advected.reshape(LEVELS, ROWS, FIELDS, LON).transpose(2, 0, 1, 3)


def solution(mesh):
    table = lane_tables()
    spec, out_spec = P("lev", "lat", "lon"), P(None, "lev", "lat", "lon")

    def run(tracers, zonal_courant, merid_courant):
        inner = functools.partial(shards, jnp.asarray(table))
        return jax.shard_map(inner, mesh=mesh, in_specs=(out_spec, spec, spec), out_specs=out_spec, check_vma=False)(
            tracers, zonal_courant, merid_courant
        )

    return run
```

profile of v0, /device:TPU:0, one launch (start us, length us, event | category | flops | bytes accessed | tf_op | source)
XLA Modules:
  0.0 37.5 jit_solution(2987491374770006627)
XLA Ops:
  0.0 1.4 %row_payload.1 = (f32[3,40,128]{2,1,0:T(8,128)S(1)}, f32[3,40,128]{2,1,0:T(8,128)S(1)}, f32[3,450,128]{2,1,0:T(8,128)S(1)}, f32[3,450,128]{2,1,0:T(8,128)S(1)}) custom-call(f32[3,1800,128]{2,1,0:T(8,128)} %bitcast.6, f32[3,450,128]{2,1,0:T(8,128)} %z_hbm.1, f32[3,450,128]{2,1,0:T(8,128)} %m_hbm.1), custom_call_target="tpu_custom_call" | custom-call | tf_op jit(solution)/shard_map/row_payload/pallas_call | solution.py:70
  1.4 3.4 %collective-permute-start.1 = (f32[3,40,128]{2,1,0:T(8,128)S(1)}, f32[3,40,128]{2,1,0:T(8,128)S(1)}, u32[]{:S(2)}, u32[]{:S(2)}) collective-permute-start(f32[3,40,128]{2,1,0:T(8,128)S(1)} %get-tuple-element.30), channel_id=1, source_target_pairs={{0,64},{2,4},{4,2},{6,70},{8,72},{10,12},{12,10},{14,78},{16,80},{... | collective-permute-start | bytes 184328 | tf_op jit(solution)/shard_map/ppermute | solution.py:547
  4.7 0.0 collective-permute-start
  4.7 2.5 %pack_middle.1 = (f32[3,2048,128]{2,1,0:T(8,128)S(1)}, f32[6,512,128]{2,1,0:T(8,128)S(1)}, f32[6,1152,128]{2,1,0:T(8,128)S(1)}, f32[2,1032,128]{2,1,0:T(8,128)S(1)}, f32[2,1032,128]{2,1,0:T(8,128)S(1)}) custom-call(f32[3,1800,128]{2,1,0:T(8,128)} %bitcast.7, f32[3,450,128]{2,1,0:T(8,128)S(1)} %get-tuple-element.22.z_ref, ...), custom_call_target="tpu_custom_call" | custom-call | tf_op jit(solution)/shard_map/pack_middle/pallas_call | solution.py:126
  7.2 0.0 collective-permute-done.1.rv
  7.2 0.0 collective-permute-done.ru
  7.2 0.0 copy-start
  7.2 0.8 %pack_rims.1 = (f32[3,2048,128]{2,1,0:T(8,128)S(1)}, f32[6,512,128]{2,1,0:T(8,128)S(1)}, f32[6,1152,128]{2,1,0:T(8,128)S(1)}, f32[2,1032,128]{2,1,0:T(8,128)S(1)...) custom-call(f32[3,2048,128]{2,1,0:T(8,128)S(1)} %get-tuple-element.2, ...), custom_call_target="tpu_custom_call", output_to_operand_aliasing={{0}: (0, {}), {1}: (1, {}), {2}: (2, {}), {3}: (3, {}), {4}... | custom-call | tf_op jit(solution)/shard_map/pack_rims/pallas_call | solution.py:204
  8.1 2.0 %collective-permute-start.2 = (f32[1104,128]{1,0:T(8,128)S(1)}, f32[1104,128]{1,0:T(8,128)S(1)}, u32[]{:S(2)}, u32[]{:S(2)}) collective-permute-start(f32[1104,128]{1,0:T(8,128)S(1)} %get-tuple-element.33), channel_id=1, source_target_pairs={{0,8},{8,16},{16,24},{24,32},{32,40},{40,48},{48,56},{56,64},{64,7... | collective-permute-start | bytes 1695752 | tf_op jit(solution)/shard_map/ppermute | solution.py:550
  10.1 4.7 %collective-permute-start.3 = (f32[1104,128]{1,0:T(8,128)S(1)}, f32[1104,128]{1,0:T(8,128)S(1)}, u32[]{:S(2)}, u32[]{:S(2)}) collective-permute-start(f32[1104,128]{1,0:T(8,128)S(1)} %get-tuple-element.34), channel_id=1, source_target_pairs={{0,120},{8,0},{16,8},{24,16},{32,24},{40,32},{48,40},{56,48},{64,5... | collective-permute-start | bytes 1695752 | tf_op jit(solution)/shard_map/ppermute | solution.py:549
  14.7 0.0 copy-done
  14.7 13.8 %inner_columns.1 = (f32[6,1152,128]{2,1,0:T(8,128)S(1)}, f32[18,160,128]{2,1,0:T(8,128)S(1)}, f32[27,64,128]{2,1,0:T(8,128)S(1)}) custom-call(f32[4,4,2,3,8,128]{5,4,3,2,1,0:T(8,128)S(1)} %copy-done, f32[6,1152,128]{2,1,0:T(8,128)S(1)} %get-tuple-element.35.d_ref, f32[2,1032,128]{2,1,0:T(8,128)S(1)} %get-tuple-element.31.cz_ref, ...), custom_call_target="tpu_custom_call", output_to_operand_aliasing={{0}: (1, {})} | custom-call | tf_op jit(solution)/shard_map/inner_columns/pallas_call | solution.py:204
  28.5 0.0 collective-permute-done.2.rw_ref
  28.5 0.0 collective-permute-done.3.re_ref
  28.6 8.9 %outer_columns.1 = f32[3,1800,128]{2,1,0:T(8,128)} custom-call(f32[4,4,2,3,8,128]{5,4,3,2,1,0:T(8,128)S(1)} %copy-done, f32[2,1032,128]{2,1,0:T(8,128)S(1)} %get-tuple-element.31.cz_ref, f32[2,1032,128]{2,1,0:T(8,128)S(1)} %get-tuple-element.32.cm_ref, f32[1104,128]{1,0:T(8,128)S(1)} %collective-permute-done.2.rw_ref, ...), custom_call_target="tpu_custom_call" | custom-call | tf_op jit(solution)/shard_map/outer_columns/pallas_call | solution.py:515
Async XLA Ops:
  1.4 5.8 %collective-permute-start.1 = (f32[3,40,128]{2,1,0:T(8,128)S(1)}, f32[3,40,128]{2,1,0:T(8,128)S(1)}, u32[]{:S(2)}, u32[]{:S(2)}) collective-permute-start(f32[3,40,128]{2,1,0:T(8,128)S(1)} %get-tuple-element.30), channel_id=1, source_target_pairs={{0,64},{2,4},{4,2},{6,70},{8,72},{10,12},{12,10},{14,78},{16,80},{... | collective-permute-start | bytes 184328 | tf_op jit(solution)/shard_map/ppermute | solution.py:547
  4.7 2.5 %collective-permute-start = (f32[3,40,128]{2,1,0:T(8,128)S(1)}, f32[3,40,128]{2,1,0:T(8,128)S(1)}, u32[]{:S(2)}, u32[]{:S(2)}) collective-permute-start(f32[3,40,128]{2,1,0:T(8,128)S(1)} %get-tuple-element.24.after_ref), channel_id=1, source_target_pairs={{0,2},{2,0},{4,6},{6,4},{8,10},{10,8},{12,14},{14,12},{16,18},{18,... | collective-permute-start | bytes 184328 | tf_op jit(solution)/shard_map/ppermute | solution.py:546
  7.2 7.5 %copy-start = (f32[4,4,2,3,8,128]{5,4,3,2,1,0:T(8,128)S(1)}, f32[4,4,2,3,8,128]{5,4,3,2,1,0:T(8,128)}, u32[]{:S(2)}) copy-start(f32[4,4,2,3,8,128]{5,4,3,2,1,0:T(8,128)} %constant.2.clone.tab) | copy-start | bytes 1179652
  8.1 20.5 %collective-permute-start.2 = (f32[1104,128]{1,0:T(8,128)S(1)}, f32[1104,128]{1,0:T(8,128)S(1)}, u32[]{:S(2)}, u32[]{:S(2)}) collective-permute-start(f32[1104,128]{1,0:T(8,128)S(1)} %get-tuple-element.33), channel_id=1, source_target_pairs={{0,8},{8,16},{16,24},{24,32},{32,40},{40,48},{48,56},{56,64},{64,7... | collective-permute-start | bytes 1695752 | tf_op jit(solution)/shard_map/ppermute | solution.py:550
  10.1 18.5 %collective-permute-start.3 = (f32[1104,128]{1,0:T(8,128)S(1)}, f32[1104,128]{1,0:T(8,128)S(1)}, u32[]{:S(2)}, u32[]{:S(2)}) collective-permute-start(f32[1104,128]{1,0:T(8,128)S(1)} %get-tuple-element.34), channel_id=1, source_target_pairs={{0,120},{8,0},{16,8},{24,16},{32,24},{40,32},{48,40},{56,48},{64,5... | collective-permute-start | bytes 1695752 | tf_op jit(solution)/shard_map/ppermute | solution.py:549
where the time goes:
time: 37.7 us; the launch traced here: 37.5 us
  Pallas kernels  27.4 us (73%)
  starting transfers between devices  10 us (27%)
    pallas_call x2, Pallas kernels, call(): pl.pallas_call(kernel, out_shape=[pltpu.VMEM(shape, jnp.float32) for shap...  14.6 us
    pallas_call x1, Pallas kernels, run_outer(): pl.pallas_call(outer_kernel, out_shape=jax.ShapeDtypeStruct((LEVELS, ROWS...  8.94 us
    ppermute x1, starting transfers between devices, shards(): lax.ppermute(to_west, 'lon', [(i, (i - 1) % LOOP) for i in range(LOOP)])  4.65 us
    ppermute x1, starting transfers between devices, shards(): rv = lax.ppermute(sv, ('lon', 'lat'), beyond)  3.36 us
    pallas_call x1, Pallas kernels, pack_middle(): pl.pallas_call(pack_middle_kernel, out_shape=[pltpu.VMEM(shape, jnp.float...  2.47 us
    ppermute x1, starting transfers between devices, shards(): lax.ppermute(to_east, 'lon', [(i, (i + 1) % LOOP) for i in range(LOOP)])  2 us
    pallas_call x1, Pallas kernels, row_payload(): pl.pallas_call(row_payload_kernel, out_shape=[pltpu.VMEM(shape, jnp.float...  1.36 us
  transfers between devices with their start and end apart: 4, of which 0 were waited for; matrix products, arithmetic and copies ran while one was open for 0% of the time, Pallas kernels for 43%

commit v1 on v0

--- a/solution.py
+++ b/solution.py
@@ -277,9 +277,13 @@
     def prepared(n, at, i):
         p = [block(s_ref, at + k, i, unroll) for k in range(3)]
         moves = [roll(p[1], 1), roll(p[2], 1), roll(p[0], 127)]
-        if band is not None:
-            moves.extend(roll(x, turn) for x in p)
-        return [(r_ref, n * 6 + slot, i, value) for slot, value in enumerate(moves)]
+        results = [(r_ref, n * 6 + slot, i, value) for slot, value in enumerate(moves)]
+        if band is not None and ahead:
+            for k in (k_first, k_first + 1):
+                results.append((r_ref, n * 6 + 3 + k, i, roll(block(s_ref, at + k, i, unroll), turn)))
+        elif band is not None:
+            results.extend((r_ref, n * 6 + 3 + k, i, roll(p[k], turn)) for k in range(3))
+        return results
 
     def store(results):
         for ref, where, i, value in results:
@@ -365,7 +369,7 @@
     spread_all(tab, band, wide, thin, c_ref, 0, (cz_ref, 0), (cm_ref, 0), ((0, LON // 8), (8, LON // 8 - 1), (8, LON // 8 - 2)))
     keep(state_ref, s_ref, 0, wide)
     keep(state_ref, s_ref, 0, thin)
-    sweeps(s_ref, c_ref, r_ref, LON // 16, 16, [(at_wide, ZONAL_WIDE, 2)])
+    sweeps(s_ref, c_ref, r_ref, 4, LON // 4 - 1, [(at_wide, ZONAL_WIDE, 2)])
 
     for cycle in range(NSTEPS):
         edge = 8 * (cycle + 1)

time: 37.7 us -> 38 us (level)
  transfers between devices with their start and end apart: 4 -> 4, of which waited for: 0 -> 0; matrix products, arithmetic and copies ran while one was open for 0% -> 0% of each run, Pallas kernels for 43% -> 44%
where the time goes in v1:
time: 38 us; the launch traced here: 37.8 us
  Pallas kernels  27.7 us (73%)
  starting transfers between devices  10 us (26%)
    pallas_call x2, Pallas kernels, call(): pl.pallas_call(kernel, out_shape=[pltpu.VMEM(shape, jnp.float32) for shap...  15 us
    pallas_call x1, Pallas kernels, run_outer(): pl.pallas_call(outer_kernel, out_shape=jax.ShapeDtypeStruct((LEVELS, ROWS...  8.94 us
    ppermute x1, starting transfers between devices, shards(): lax.ppermute(to_west, 'lon', [(i, (i - 1) % LOOP) for i in range(LOOP)])  4.65 us
    ppermute x1, starting transfers between devices, shards(): rv = lax.ppermute(sv, ('lon', 'lat'), beyond)  3.36 us
    pallas_call x1, Pallas kernels, pack_middle(): pl.pallas_call(pack_middle_kernel, out_shape=[pltpu.VMEM(shape, jnp.float...  2.47 us
    ppermute x1, starting transfers between devices, shards(): lax.ppermute(to_east, 'lon', [(i, (i + 1) % LOOP) for i in range(LOOP)])  2 us
    pallas_call x1, Pallas kernels, row_payload(): pl.pallas_call(row_payload_kernel, out_shape=[pltpu.VMEM(shape, jnp.float...  1.36 us
  transfers between devices with their start and end apart: 4, of which 0 were waited for; matrix products, arithmetic and copies ran while one was open for 0% of the time, Pallas kernels for 44%

profile of v1, /device:TPU:0, one launch (start us, length us, event | category | flops | bytes accessed | tf_op | source)
XLA Modules:
  0.0 37.8 jit_solution(13534217839237584599)
XLA Ops:
  0.0 1.4 %row_payload.1 = (f32[3,40,128]{2,1,0:T(8,128)S(1)}, f32[3,40,128]{2,1,0:T(8,128)S(1)}, f32[3,450,128]{2,1,0:T(8,128)S(1)}, f32[3,450,128]{2,1,0:T(8,128)S(1)}) custom-call(f32[3,1800,128]{2,1,0:T(8,128)} %bitcast.6, f32[3,450,128]{2,1,0:T(8,128)} %z_hbm.1, f32[3,450,128]{2,1,0:T(8,128)} %m_hbm.1), custom_call_target="tpu_custom_call" | custom-call | tf_op jit(solution)/shard_map/row_payload/pallas_call | solution.py:70
  1.4 3.4 %collective-permute-start.1 = (f32[3,40,128]{2,1,0:T(8,128)S(1)}, f32[3,40,128]{2,1,0:T(8,128)S(1)}, u32[]{:S(2)}, u32[]{:S(2)}) collective-permute-start(f32[3,40,128]{2,1,0:T(8,128)S(1)} %get-tuple-element.30), channel_id=1, source_target_pairs={{0,64},{2,4},{4,2},{6,70},{8,72},{10,12},{12,10},{14,78},{16,80},{... | collective-permute-start | bytes 184328 | tf_op jit(solution)/shard_map/ppermute | solution.py:551
  4.7 0.0 collective-permute-start
  4.7 2.5 %pack_middle.1 = (f32[3,2048,128]{2,1,0:T(8,128)S(1)}, f32[6,512,128]{2,1,0:T(8,128)S(1)}, f32[6,1152,128]{2,1,0:T(8,128)S(1)}, f32[2,1032,128]{2,1,0:T(8,128)S(1)}, f32[2,1032,128]{2,1,0:T(8,128)S(1)}) custom-call(f32[3,1800,128]{2,1,0:T(8,128)} %bitcast.7, f32[3,450,128]{2,1,0:T(8,128)S(1)} %get-tuple-element.22.z_ref, ...), custom_call_target="tpu_custom_call" | custom-call | tf_op jit(solution)/shard_map/pack_middle/pallas_call | solution.py:126
  7.2 0.0 collective-permute-done.1.rv
  7.2 0.0 collective-permute-done.ru
  7.2 0.0 copy-start
  7.2 0.8 %pack_rims.1 = (f32[3,2048,128]{2,1,0:T(8,128)S(1)}, f32[6,512,128]{2,1,0:T(8,128)S(1)}, f32[6,1152,128]{2,1,0:T(8,128)S(1)}, f32[2,1032,128]{2,1,0:T(8,128)S(1)...) custom-call(f32[3,2048,128]{2,1,0:T(8,128)S(1)} %get-tuple-element.2, ...), custom_call_target="tpu_custom_call", output_to_operand_aliasing={{0}: (0, {}), {1}: (1, {}), {2}: (2, {}), {3}: (3, {}), {4}... | custom-call | tf_op jit(solution)/shard_map/pack_rims/pallas_call | solution.py:204
  8.1 2.0 %collective-permute-start.2 = (f32[1104,128]{1,0:T(8,128)S(1)}, f32[1104,128]{1,0:T(8,128)S(1)}, u32[]{:S(2)}, u32[]{:S(2)}) collective-permute-start(f32[1104,128]{1,0:T(8,128)S(1)} %get-tuple-element.33), channel_id=1, source_target_pairs={{0,8},{8,16},{16,24},{24,32},{32,40},{40,48},{48,56},{56,64},{64,7... | collective-permute-start | bytes 1695752 | tf_op jit(solution)/shard_map/ppermute | solution.py:554
  10.1 4.7 %collective-permute-start.3 = (f32[1104,128]{1,0:T(8,128)S(1)}, f32[1104,128]{1,0:T(8,128)S(1)}, u32[]{:S(2)}, u32[]{:S(2)}) collective-permute-start(f32[1104,128]{1,0:T(8,128)S(1)} %get-tuple-element.34), channel_id=1, source_target_pairs={{0,120},{8,0},{16,8},{24,16},{32,24},{40,32},{48,40},{56,48},{64,5... | collective-permute-start | bytes 1695752 | tf_op jit(solution)/shard_map/ppermute | solution.py:553
  14.7 0.0 copy-done
  14.7 14.1 %inner_columns.1 = (f32[6,1152,128]{2,1,0:T(8,128)S(1)}, f32[18,160,128]{2,1,0:T(8,128)S(1)}, f32[27,64,128]{2,1,0:T(8,128)S(1)}) custom-call(f32[4,4,2,3,8,128]{5,4,3,2,1,0:T(8,128)S(1)} %copy-done, f32[6,1152,128]{2,1,0:T(8,128)S(1)} %get-tuple-element.35.d_ref, f32[2,1032,128]{2,1,0:T(8,128)S(1)} %get-tuple-element.31.cz_ref, ...), custom_call_target="tpu_custom_call", output_to_operand_aliasing={{0}: (1, {})} | custom-call | tf_op jit(solution)/shard_map/inner_columns/pallas_call | solution.py:204
  28.9 0.0 collective-permute-done.2.rw_ref
  28.9 0.0 collective-permute-done.3.re_ref
  28.9 8.9 %outer_columns.1 = f32[3,1800,128]{2,1,0:T(8,128)} custom-call(f32[4,4,2,3,8,128]{5,4,3,2,1,0:T(8,128)S(1)} %copy-done, f32[2,1032,128]{2,1,0:T(8,128)S(1)} %get-tuple-element.31.cz_ref, f32[2,1032,128]{2,1,0:T(8,128)S(1)} %get-tuple-element.32.cm_ref, f32[1104,128]{1,0:T(8,128)S(1)} %collective-permute-done.2.rw_ref, ...), custom_call_target="tpu_custom_call" | custom-call | tf_op jit(solution)/shard_map/outer_columns/pallas_call | solution.py:519
Async XLA Ops:
  1.4 5.8 %collective-permute-start.1 = (f32[3,40,128]{2,1,0:T(8,128)S(1)}, f32[3,40,128]{2,1,0:T(8,128)S(1)}, u32[]{:S(2)}, u32[]{:S(2)}) collective-permute-start(f32[3,40,128]{2,1,0:T(8,128)S(1)} %get-tuple-element.30), channel_id=1, source_target_pairs={{0,64},{2,4},{4,2},{6,70},{8,72},{10,12},{12,10},{14,78},{16,80},{... | collective-permute-start | bytes 184328 | tf_op jit(solution)/shard_map/ppermute | solution.py:551
  4.7 2.5 %collective-permute-start = (f32[3,40,128]{2,1,0:T(8,128)S(1)}, f32[3,40,128]{2,1,0:T(8,128)S(1)}, u32[]{:S(2)}, u32[]{:S(2)}) collective-permute-start(f32[3,40,128]{2,1,0:T(8,128)S(1)} %get-tuple-element.24.after_ref), channel_id=1, source_target_pairs={{0,2},{2,0},{4,6},{6,4},{8,10},{10,8},{12,14},{14,12},{16,18},{18,... | collective-permute-start | bytes 184328 | tf_op jit(solution)/shard_map/ppermute | solution.py:550
  7.2 7.5 %copy-start = (f32[4,4,2,3,8,128]{5,4,3,2,1,0:T(8,128)S(1)}, f32[4,4,2,3,8,128]{5,4,3,2,1,0:T(8,128)}, u32[]{:S(2)}) copy-start(f32[4,4,2,3,8,128]{5,4,3,2,1,0:T(8,128)} %constant.2.clone.tab) | copy-start | bytes 1179652
  8.1 20.8 %collective-permute-start.2 = (f32[1104,128]{1,0:T(8,128)S(1)}, f32[1104,128]{1,0:T(8,128)S(1)}, u32[]{:S(2)}, u32[]{:S(2)}) collective-permute-start(f32[1104,128]{1,0:T(8,128)S(1)} %get-tuple-element.33), channel_id=1, source_target_pairs={{0,8},{8,16},{16,24},{24,32},{32,40},{40,48},{48,56},{56,64},{64,7... | collective-permute-start | bytes 1695752 | tf_op jit(solution)/shard_map/ppermute | solution.py:554
  10.1 18.8 %collective-permute-start.3 = (f32[1104,128]{1,0:T(8,128)S(1)}, f32[1104,128]{1,0:T(8,128)S(1)}, u32[]{:S(2)}, u32[]{:S(2)}) collective-permute-start(f32[1104,128]{1,0:T(8,128)S(1)} %get-tuple-element.34), channel_id=1, source_target_pairs={{0,120},{8,0},{16,8},{24,16},{32,24},{40,32},{48,40},{56,48},{64,5... | collective-permute-start | bytes 1695752 | tf_op jit(solution)/shard_map/ppermute | solution.py:553

commit v2 on v1

--- a/solution.py
+++ b/solution.py
@@ -369,7 +369,7 @@
     spread_all(tab, band, wide, thin, c_ref, 0, (cz_ref, 0), (cm_ref, 0), ((0, LON // 8), (8, LON // 8 - 1), (8, LON // 8 - 2)))
     keep(state_ref, s_ref, 0, wide)
     keep(state_ref, s_ref, 0, thin)
-    sweeps(s_ref, c_ref, r_ref, 4, LON // 4 - 1, [(at_wide, ZONAL_WIDE, 2)])
+    sweeps(s_ref, c_ref, r_ref, LON // 16, 16, [(at_wide, ZONAL_WIDE, 2)])
 
     for cycle in range(NSTEPS):
         edge = 8 * (cycle + 1)

time: 38 us -> 38 us (level)
  no operation moved by 1% of the time
where the time goes in v2:
time: 38 us; the launch traced here: 37.9 us
  Pallas kernels  27.8 us (73%)
  starting transfers between devices  10 us (26%)
    pallas_call x2, Pallas kernels, call(): pl.pallas_call(kernel, out_shape=[pltpu.VMEM(shape, jnp.float32) for shap...  15 us
    pallas_call x1, Pallas kernels, run_outer(): pl.pallas_call(outer_kernel, out_shape=jax.ShapeDtypeStruct((LEVELS, ROWS...  8.94 us
    ppermute x1, starting transfers between devices, shards(): lax.ppermute(to_west, 'lon', [(i, (i - 1) % LOOP) for i in range(LOOP)])  4.65 us
    ppermute x1, starting transfers between devices, shards(): rv = lax.ppermute(sv, ('lon', 'lat'), beyond)  3.36 us
    pallas_call x1, Pallas kernels, pack_middle(): pl.pallas_call(pack_middle_kernel, out_shape=[pltpu.VMEM(shape, jnp.float...  2.47 us
    ppermute x1, starting transfers between devices, shards(): lax.ppermute(to_east, 'lon', [(i, (i + 1) % LOOP) for i in range(LOOP)])  2 us
    pallas_call x1, Pallas kernels, row_payload(): pl.pallas_call(row_payload_kernel, out_shape=[pltpu.VMEM(shape, jnp.float...  1.36 us
  transfers between devices with their start and end apart: 4, of which 0 were waited for; matrix products, arithmetic and copies ran while one was open for 0% of the time, Pallas kernels for 44%

profile of v2, /device:TPU:0, one launch (start us, length us, event | category | flops | bytes accessed | tf_op | source)
XLA Modules:
  0.0 37.9 jit_solution(8630223614194120110)
XLA Ops:
  0.0 1.4 %row_payload.1 = (f32[3,40,128]{2,1,0:T(8,128)S(1)}, f32[3,40,128]{2,1,0:T(8,128)S(1)}, f32[3,450,128]{2,1,0:T(8,128)S(1)}, f32[3,450,128]{2,1,0:T(8,128)S(1)}) custom-call(f32[3,1800,128]{2,1,0:T(8,128)} %bitcast.6, f32[3,450,128]{2,1,0:T(8,128)} %z_hbm.1, f32[3,450,128]{2,1,0:T(8,128)} %m_hbm.1), custom_call_target="tpu_custom_call" | custom-call | tf_op jit(solution)/shard_map/row_payload/pallas_call | solution.py:70
  1.4 3.4 %collective-permute-start.1 = (f32[3,40,128]{2,1,0:T(8,128)S(1)}, f32[3,40,128]{2,1,0:T(8,128)S(1)}, u32[]{:S(2)}, u32[]{:S(2)}) collective-permute-start(f32[3,40,128]{2,1,0:T(8,128)S(1)} %get-tuple-element.30), channel_id=1, source_target_pairs={{0,64},{2,4},{4,2},{6,70},{8,72},{10,12},{12,10},{14,78},{16,80},{... | collective-permute-start | bytes 184328 | tf_op jit(solution)/shard_map/ppermute | solution.py:551
  4.7 0.0 collective-permute-start
  4.7 2.5 %pack_middle.1 = (f32[3,2048,128]{2,1,0:T(8,128)S(1)}, f32[6,512,128]{2,1,0:T(8,128)S(1)}, f32[6,1152,128]{2,1,0:T(8,128)S(1)}, f32[2,1032,128]{2,1,0:T(8,128)S(1)}, f32[2,1032,128]{2,1,0:T(8,128)S(1)}) custom-call(f32[3,1800,128]{2,1,0:T(8,128)} %bitcast.7, f32[3,450,128]{2,1,0:T(8,128)S(1)} %get-tuple-element.22.z_ref, ...), custom_call_target="tpu_custom_call" | custom-call | tf_op jit(solution)/shard_map/pack_middle/pallas_call | solution.py:126
  7.2 0.0 collective-permute-done.1.rv
  7.2 0.0 collective-permute-done.ru
  7.2 0.0 copy-start
  7.2 0.8 %pack_rims.1 = (f32[3,2048,128]{2,1,0:T(8,128)S(1)}, f32[6,512,128]{2,1,0:T(8,128)S(1)}, f32[6,1152,128]{2,1,0:T(8,128)S(1)}, f32[2,1032,128]{2,1,0:T(8,128)S(1)...) custom-call(f32[3,2048,128]{2,1,0:T(8,128)S(1)} %get-tuple-element.2, ...), custom_call_target="tpu_custom_call", output_to_operand_aliasing={{0}: (0, {}), {1}: (1, {}), {2}: (2, {}), {3}: (3, {}), {4}... | custom-call | tf_op jit(solution)/shard_map/pack_rims/pallas_call | solution.py:204
  8.1 2.0 %collective-permute-start.2 = (f32[1104,128]{1,0:T(8,128)S(1)}, f32[1104,128]{1,0:T(8,128)S(1)}, u32[]{:S(2)}, u32[]{:S(2)}) collective-permute-start(f32[1104,128]{1,0:T(8,128)S(1)} %get-tuple-element.33), channel_id=1, source_target_pairs={{0,8},{8,16},{16,24},{24,32},{32,40},{40,48},{48,56},{56,64},{64,7... | collective-permute-start | bytes 1695752 | tf_op jit(solution)/shard_map/ppermute | solution.py:554
  10.1 4.7 %collective-permute-start.3 = (f32[1104,128]{1,0:T(8,128)S(1)}, f32[1104,128]{1,0:T(8,128)S(1)}, u32[]{:S(2)}, u32[]{:S(2)}) collective-permute-start(f32[1104,128]{1,0:T(8,128)S(1)} %get-tuple-element.34), channel_id=1, source_target_pairs={{0,120},{8,0},{16,8},{24,16},{32,24},{40,32},{48,40},{56,48},{64,5... | collective-permute-start | bytes 1695752 | tf_op jit(solution)/shard_map/ppermute | solution.py:553
  14.7 0.0 copy-done
  14.7 14.2 %inner_columns.1 = (f32[6,1152,128]{2,1,0:T(8,128)S(1)}, f32[18,160,128]{2,1,0:T(8,128)S(1)}, f32[27,64,128]{2,1,0:T(8,128)S(1)}) custom-call(f32[4,4,2,3,8,128]{5,4,3,2,1,0:T(8,128)S(1)} %copy-done, f32[6,1152,128]{2,1,0:T(8,128)S(1)} %get-tuple-element.35.d_ref, f32[2,1032,128]{2,1,0:T(8,128)S(1)} %get-tuple-element.31.cz_ref, ...), custom_call_target="tpu_custom_call", output_to_operand_aliasing={{0}: (1, {})} | custom-call | tf_op jit(solution)/shard_map/inner_columns/pallas_call | solution.py:204
  28.9 0.0 collective-permute-done.2.rw_ref
  28.9 0.0 collective-permute-done.3.re_ref
  28.9 8.9 %outer_columns.1 = f32[3,1800,128]{2,1,0:T(8,128)} custom-call(f32[4,4,2,3,8,128]{5,4,3,2,1,0:T(8,128)S(1)} %copy-done, f32[2,1032,128]{2,1,0:T(8,128)S(1)} %get-tuple-element.31.cz_ref, f32[2,1032,128]{2,1,0:T(8,128)S(1)} %get-tuple-element.32.cm_ref, f32[1104,128]{1,0:T(8,128)S(1)} %collective-permute-done.2.rw_ref, ...), custom_call_target="tpu_custom_call" | custom-call | tf_op jit(solution)/shard_map/outer_columns/pallas_call | solution.py:519
Async XLA Ops:
  1.4 5.8 %collective-permute-start.1 = (f32[3,40,128]{2,1,0:T(8,128)S(1)}, f32[3,40,128]{2,1,0:T(8,128)S(1)}, u32[]{:S(2)}, u32[]{:S(2)}) collective-permute-start(f32[3,40,128]{2,1,0:T(8,128)S(1)} %get-tuple-element.30), channel_id=1, source_target_pairs={{0,64},{2,4},{4,2},{6,70},{8,72},{10,12},{12,10},{14,78},{16,80},{... | collective-permute-start | bytes 184328 | tf_op jit(solution)/shard_map/ppermute | solution.py:551
  4.7 2.5 %collective-permute-start = (f32[3,40,128]{2,1,0:T(8,128)S(1)}, f32[3,40,128]{2,1,0:T(8,128)S(1)}, u32[]{:S(2)}, u32[]{:S(2)}) collective-permute-start(f32[3,40,128]{2,1,0:T(8,128)S(1)} %get-tuple-element.24.after_ref), channel_id=1, source_target_pairs={{0,2},{2,0},{4,6},{6,4},{8,10},{10,8},{12,14},{14,12},{16,18},{18,... | collective-permute-start | bytes 184328 | tf_op jit(solution)/shard_map/ppermute | solution.py:550
  7.2 7.5 %copy-start = (f32[4,4,2,3,8,128]{5,4,3,2,1,0:T(8,128)S(1)}, f32[4,4,2,3,8,128]{5,4,3,2,1,0:T(8,128)}, u32[]{:S(2)}) copy-start(f32[4,4,2,3,8,128]{5,4,3,2,1,0:T(8,128)} %constant.2.clone.tab) | copy-start | bytes 1179652
  8.1 20.8 %collective-permute-start.2 = (f32[1104,128]{1,0:T(8,128)S(1)}, f32[1104,128]{1,0:T(8,128)S(1)}, u32[]{:S(2)}, u32[]{:S(2)}) collective-permute-start(f32[1104,128]{1,0:T(8,128)S(1)} %get-tuple-element.33), channel_id=1, source_target_pairs={{0,8},{8,16},{16,24},{24,32},{32,40},{40,48},{48,56},{56,64},{64,7... | collective-permute-start | bytes 1695752 | tf_op jit(solution)/shard_map/ppermute | solution.py:554
  10.1 18.9 %collective-permute-start.3 = (f32[1104,128]{1,0:T(8,128)S(1)}, f32[1104,128]{1,0:T(8,128)S(1)}, u32[]{:S(2)}, u32[]{:S(2)}) collective-permute-start(f32[1104,128]{1,0:T(8,128)S(1)} %get-tuple-element.34), channel_id=1, source_target_pairs={{0,120},{8,0},{16,8},{24,16},{32,24},{40,32},{48,40},{56,48},{64,5... | collective-permute-start | bytes 1695752 | tf_op jit(solution)/shard_map/ppermute | solution.py:553
